TPU v7x, 256 devices: a whole 4x4x8 slice. The times are simulated.
256 devices in a mesh: store: 64 (over z, y, core), tp: 4 (over x).
Axes of the slice: x: 4, y: 4, z: 8, core: 2. Of those that a mesh axis runs over, the one named last changes fastest.
Arguments:
- query_embeds: bfloat16 [128, 16, 4096], P('store', None, 'tp'), may hold values from -6 to 6
- passage_embeds: bfloat16 [128, 32, 4096], P('store', None, 'tp'), may hold values from -6 to 6
- passage_lengths: int32 [128], P('store'), may hold values from 1 to 32, as said below
- cand_passage: int32 [1536], P('store'), may hold values from 0 to 127, as said below
- norm_gain: bfloat16 [4096], replicated, may hold values from 0.099609375 to 1.8984375
- w_qkv: bfloat16 [4096, 16, 384], P(None, 'tp'), may hold values from -1 to 1
Outputs:
- query_attn: bfloat16 [128, 16, 2048], P('store', None, 'tp')
- passage_attn: bfloat16 [1536, 32, 2048], P('store', None, 'tp')
Inputs may be any that keep to these rules, and one draw needn't show every extreme that they name: `cand_passage`: passage id p is held by store index p // 2 at position p % 2. Among the 24 pairs of one store index, the passages come from as many different store indices as possible, and no store index holds the passages of more than 1 of them. `passage_lengths`: some passage has 32 tokens.
All inputs are finite; a program needn't handle non-finite values.
Results may differ from a plain program's by a relative error of at most 0.023.
The roundings to bfloat16 on the way count: a program that leaves them out, or rounds other values in their place, can miss the bound.
Values may be sent and summed in bfloat16 or wider, within the bound.
A program may use at most 128 MiB of HBM per device.

v0:
```python
import math
import jax
import jax.numpy as jnp
from jax import lax
from jax.sharding import PartitionSpec as P


def rms_rows(rows, norm_gain):
    values = rows.astype(jnp.float32)
    meansq = jnp.mean(values * values, axis=-1, keepdims=True)
    scaled = values * lax.rsqrt(meansq + 1e-05) * norm_gain.astype(jnp.float32)
    return scaled.astype(jnp.bfloat16)


def rotate_parts(raw, positions, head_dim):
    half_dim = head_dim // 2
    inverse = jnp.exp(
        jnp.arange(half_dim, dtype=jnp.float32) * (-2.0 * math.log(10000.0) / head_dim)
    )
    angles = positions[:, None] * inverse[None, :]
    cosine = jnp.cos(angles)[:, None, :]
    sine_part = jnp.sin(angles)[:, None, :]

    def turned(block):
        first = block[..., :half_dim]
        second = block[..., half_dim:]
        return jnp.concatenate(
            [first * cosine - second * sine_part, second * cosine + first * sine_part], axis=-1
        )

    queries = turned(raw[..., :head_dim])
    keyset = turned(raw[..., head_dim : 2 * head_dim])
    values = raw[..., 2 * head_dim :]
    return jnp.concatenate([queries, keyset, values], axis=-1).astype(jnp.bfloat16)


def softmax_rounded(scores, allowed):
    masked = jnp.where(allowed, scores, jnp.float32(-1e30))
    peak = jnp.max(masked, axis=-1, keepdims=True)
    expon = jnp.where(allowed, jnp.exp(masked - peak), jnp.float32(0.0))
    return (expon / jnp.sum(expon, axis=-1, keepdims=True)).astype(jnp.bfloat16)


def attend_queries(query_qkv, head_dim):
    count, query_len, heads = (query_qkv.shape[0], query_qkv.shape[1], query_qkv.shape[2])
    scale = head_dim ** (-0.5)
    scores = (
        jnp.einsum(
            "bqhd,bkhd->bhqk",
            query_qkv[..., :head_dim],
            query_qkv[..., head_dim : 2 * head_dim],
            preferred_element_type=jnp.float32,
        )
        * scale
    )
    steps_row = jnp.arange(query_len, dtype=jnp.int32)
    allowed = steps_row[:, None] >= steps_row[None, :]
    weights = softmax_rounded(scores, allowed[None, None])
    output = jnp.einsum(
        "bhqk,bkhd->bqhd",
        weights,
        query_qkv[..., 2 * head_dim :],
        preferred_element_type=jnp.float32,
    )
    return output.reshape(count, query_len, heads * head_dim).astype(jnp.bfloat16)


def attend_core(query_kv, pair_qkv, pair_lengths, head_dim):
    query_len = query_kv.shape[1]
    pairs, passage_len, heads = (pair_qkv.shape[0], pair_qkv.shape[1], pair_qkv.shape[2])
    scale = head_dim ** (-0.5)
    keyset = jnp.concatenate(
        [query_kv[..., :head_dim], pair_qkv[..., head_dim : 2 * head_dim]], axis=1
    )
    values = jnp.concatenate([query_kv[..., head_dim:], pair_qkv[..., 2 * head_dim :]], axis=1)
    scores = (
        jnp.einsum(
            "bihd,bthd->bhit", pair_qkv[..., :head_dim], keyset, preferred_element_type=jnp.float32
        )
        * scale
    )
    column = jnp.arange(query_len + passage_len, dtype=jnp.int32) - query_len
    row_index = jnp.arange(passage_len, dtype=jnp.int32)
    allowed = (column[None, None, :] < 0) | (column[None, None, :] <= row_index[None, :, None]) & (
        column[None, None, :] < pair_lengths[:, None, None]
    )
    weights = softmax_rounded(scores, allowed[:, None])
    output = jnp.einsum("bhit,bthd->bihd", weights, values, preferred_element_type=jnp.float32)
    live = row_index[None, :] < pair_lengths[:, None]
    output = jnp.where(live[:, :, None, None], output, jnp.float32(0.0))
    return output.reshape(pairs, passage_len, heads * head_dim).astype(jnp.bfloat16)


def attend_pairs(query_qkv, pair_qkv, pair_lengths, head_dim, cands):
    repeated = jnp.repeat(query_qkv[..., head_dim:], cands, axis=0)
    return attend_core(repeated, pair_qkv, pair_lengths, head_dim)


def local(query_embeds, passage_embeds, passage_lengths, cand_passage, norm_gain, w_qkv):
    n_store = lax.axis_size("store")
    quer_count, query_len, width_part = query_embeds.shape
    pass_count, passage_len = (passage_embeds.shape[0], passage_embeds.shape[1])
    pairs_dev = cand_passage.shape[0]
    cands = pairs_dev // quer_count
    heads_part = w_qkv.shape[1]
    head_dim = w_qkv.shape[2] // 3
    capacity = (pairs_dev + n_store - 1) // n_store
    weights_flat = w_qkv.reshape(w_qkv.shape[0], heads_part * 3 * head_dim)
    query_rows = query_embeds.reshape(quer_count * query_len, width_part)
    query_pos = jnp.tile(jnp.arange(query_len, dtype=jnp.float32), quer_count)
    query_total = quer_count * query_len
    holder = cand_passage // pass_count
    same_holder = holder[:, None] == holder[None, :]
    pair_index = jnp.arange(pairs_dev, dtype=jnp.int32)
    earlier = pair_index[:, None] < pair_index[None, :]
    rank_in = jnp.sum((same_holder & earlier).astype(jnp.int32), axis=0)
    slot_code = cand_passage % pass_count + 1
    hits = (holder[:, None, None] == jnp.arange(n_store, dtype=jnp.int32)[None, :, None]) & (
        rank_in[:, None, None] == jnp.arange(capacity, dtype=jnp.int32)[None, None, :]
    )
    request = jnp.sum(jnp.where(hits, slot_code[:, None, None], 0), axis=0)
    flat_index = holder * capacity + rank_in
    hits, request, flat_index = (hits, request, flat_index)
    incoming = lax.all_to_all(request, "store", split_axis=0, concat_axis=0, tiled=True)
    chosen = jnp.maximum(incoming - 1, 0)
    filled = incoming > 0
    outgoing = jnp.where(
        filled[:, :, None, None], passage_embeds[chosen], jnp.zeros((), passage_embeds.dtype)
    )
    out_len = jnp.where(filled, passage_lengths[chosen], 0)
    arrived = lax.all_to_all(outgoing, "store", split_axis=0, concat_axis=0, tiled=True)
    arrived_len = lax.all_to_all(out_len, "store", split_axis=0, concat_axis=0, tiled=True)
    flat_rows = arrived.reshape((n_store * capacity,) + passage_embeds.shape[1:])
    fetched = flat_rows[flat_index]
    pair_lengths = arrived_len.reshape(n_store * capacity)[flat_index]
    pair_pos = query_len + jnp.tile(jnp.arange(passage_len, dtype=jnp.float32), pairs_dev)
    all_rows = jnp.concatenate(
        [query_rows, fetched.reshape(pairs_dev * passage_len, width_part)], axis=0
    )
    full_rows = lax.all_gather(all_rows, "tp", axis=1, tiled=True)
    normed = rms_rows(full_rows, norm_gain)
    raw = jnp.dot(normed, weights_flat, preferred_element_type=jnp.float32)
    raw = raw.reshape(all_rows.shape[0], heads_part, 3 * head_dim)
    projected = rotate_parts(raw, jnp.concatenate([query_pos, pair_pos], axis=0), head_dim)
    query_qkv = projected[:query_total].reshape(quer_count, query_len, heads_part, 3 * head_dim)
    pair_qkv = projected[query_total:].reshape(pairs_dev, passage_len, heads_part, 3 * head_dim)
    query_attn = attend_queries(query_qkv, head_dim)
    passage_attn = attend_pairs(query_qkv, pair_qkv, pair_lengths, head_dim, cands)
    return (query_attn, passage_attn)


def solution(mesh):
    in_specs = (
        P("store", None, "tp"),
        P("store", None, "tp"),
        P("store"),
        P("store"),
        P(),
        P(None, "tp", None),
    )
    out_specs = (P("store", None, "tp"), P("store", None, "tp"))
    return jax.shard_map(local, mesh=mesh, in_specs=in_specs, out_specs=out_specs, check_vma=False)
```

profile of v0, /device:TPU:1, one launch (start us, length us, event | category | flops | bytes accessed | tf_op | source)
XLA Modules:
  0.0 256.2 jit_solution(16776355402907766415)
XLA Ops:
  7.2 0.0 copy-start
  7.2 0.7 and_select_fusion.1
  7.9 0.1 convert_reduce_fusion
  8.0 0.1 select_reduce_fusion
  8.1 0.7 copy.58
  8.8 13.2 %all-to-all-start = ((s32[64,1,1]{2,1,0:T(1,128)}), s32[64,1,1]{2,1,0:T(1,128)S(1)}, u32[]{:S(2)}, u32[]{:S(2)}) async-start(s32[64,1,1]{2,1,0:T(1,128)} %copy.58), calls=%async_computation | async-start | bytes 65536 | tf_op jit(solution)/shard_map/all_to_all | solution.py:124
  22.0 1.3 fusion.51
  23.3 8.0 %all-to-all-done = s32[64,1,1]{2,1,0:T(1,128)S(1)} async-done(((s32[64,1,1]{2,1,0:T(1,128)}), s32[64,1,1]{2,1,0:T(1,128)S(1)}, u32[]{:S(2)}, u32[]{:S(2)}) %all-to-all-start) | async-done | bytes 288 | tf_op jit(solution)/shard_map/all_to_all | solution.py:124
  31.3 0.1 copy.59
  31.3 1.3 compare_select_fusion.5
  32.6 0.0 copy-done
  32.6 2.8 %gather_fusion = bf16[64,32,1024]{2,1,0:T(8,128)(2,1)} fusion(bf16[2,32,1024]{2,1,0:T(8,128)(2,1)S(1)} %copy-done, s32[1024]{0:T(1024)S(1)} %pad_clamp_fusion.1), kind=kCustom, calls=%fused_computation | custom fusion | bytes 8388864 | tf_op jit(solution)/shard_map/gather | solution.py:128
  35.4 4.5 %bitcast_select_fusion = bf16[64,1,32,1024]{3,2,1,0:T(8,128)(2,1)} fusion(bf16[64,32,1024]{2,1,0:T(8,128)(2,1)} %gather_fusion, pred[64]{0:T(512)(128)(4,1)S(1)} %compare_bitcast_fusion), kind=kLoop, calls=%fused_computation.14 | loop fusion | flops 2097152 | bytes 8388672 | tf_op jit(solution)/shard_map/jit(_where)/select_n | solution.py:127
  39.9 5.7 %all-to-all-start.1 = ((bf16[64,1,32,1024]{3,2,1,0:T(8,128)(2,1)}), bf16[64,1,32,1024]{3,2,1,0:T(8,128)(2,1)}, u32[]{:S(2)}, u32[]{:S(2)}) async-start(bf16[64,1,32,1024]{3,2,1,0:T(8,128)(2,1)} %bitcast_select_fusion), calls=%async_computation.1 | async-start | bytes 8388608 | tf_op jit(solution)/shard_map/all_to_all | solution.py:131
  45.6 0.0 copy-start.5
  45.6 0.0 all-gather.2.cloned.1.call-start
  45.7 94.6 %all-to-all-done.1 = bf16[64,1,32,1024]{3,2,1,0:T(8,128)(2,1)} async-done(((bf16[64,1,32,1024]{3,2,1,0:T(8,128)(2,1)}), bf16[64,1,32,1024]{3,2,1,0:T(8,128)(2,1)}, u32[]{:S(2)}, u32[]{:S(2)}) %all-to-all-start.1) | async-done | bytes 4194336 | tf_op jit(solution)/shard_map/all_to_all | solution.py:131
  140.3 2.8 %gather_fusion.1 = bf16[24,32,1024]{2,1,0:T(8,128)(2,1)S(1)} fusion(bf16[64,32,1024]{2,1,0:T(8,128)(2,1)} %bitcast.5, s32[1024]{0:T(1024)S(1)} %pad_clamp_fusion), kind=kCustom, calls=%fused_computation.1 | custom fusion | bytes 3145824 | tf_op jit(solution)/shard_map/gather | solution.py:134
  143.1 0.0 copy-done.5
  143.1 1.3 pad_maximum_fusion
  144.4 0.0 all-gather.2.cloned.1.call-update
  144.5 0.1 add.65
  144.6 0.1 tile.7
  144.7 0.1 pad_maximum_fusion.1
  144.7 1.5 multiply_cosine_fusion
  146.2 0.7 copy.67
  147.0 7.0 %all-to-all-start.2 = ((s32[64,1,1]{2,1,0:T(1,128)}), s32[64,1,1]{2,1,0:T(1,128)S(1)}, u32[]{:S(2)}, u32[]{:S(2)}) async-start(s32[64,1,1]{2,1,0:T(1,128)} %copy.67), calls=%async_computation.2 | async-start | bytes 65536 | tf_op jit(solution)/shard_map/all_to_all | solution.py:132
  154.0 12.9 %copy.82 = bf16[512,8,4,384]{3,1,2,0:T(8,128)(2,1)} copy(bf16[512,8,4,384]{3,2,1,0:T(4,128)(2,1)} %bitcast.43) | data formatting | bytes 25165824
  166.9 0.0 copy-start.6
  166.9 16.7 %copy.61 = bf16[1536,4096]{1,0:T(8,128)(2,1)} copy(bf16[1536,4096]{0,1:T(8,128)(2,1)} %bitcast.42) | data formatting | bytes 25165824 | tf_op jit(solution)/shard_map/dot_general | solution.py:142
  183.6 0.0 copy-done.6
  183.6 0.0 all-to-all-done.2
  183.6 1.2 reduce.1
  184.9 0.7 gather_fusion.2
  185.6 0.1 iota_compare_fusion.1
  185.6 0.1 broadcast_compare_fusion
  185.7 0.1 and_or_fusion
  185.8 26.8 %all-gather.2.cloned.1.call-done = bf16[800,4096]{1,0:T(8,128)(2,1)} async-done(((bf16[800,1024]{1,0:T(8,128)(2,1)}), bf16[800,4096]{1,0:T(8,128)(2,1)}) %all-gather.2.cloned.1.call-update) | async-done | bytes 6553616 | tf_op jit(solution)/shard_map/all_gather | solution.py:140
  212.6 0.0 copy-start.3
  212.6 4.4 %fusion.2 = f32[800]{0:T(1024)S(1)} fusion(bf16[800,4096]{1,0:T(8,128)(2,1)} %all-gather.2.cloned.1.call-done), kind=kLoop, calls=%fused_computation.7 | loop fusion | flops 9829600 | bytes 6556800 | tf_op jit(solution)/shard_map/reduce_sum | solution.py:10
  217.0 0.4 copy-done.3
  217.4 13.5 %fusion.6 = f32[800,4,384]{2,0,1:T(8,128)S(1)} fusion(bf16[4,384,4096]{2,1,0:T(8,128)(2,1)} %bitcast.44, bf16[800,4096]{1,0:T(8,128)(2,1)S(1)} %copy-done.3, f32[4096]{0:T(1024)S(1)} %convert_element_type.39, f32[800]{0:T(1024)S(1)} %add_rsqrt_fusion), kind=kOutput, calls=%fused_computation.11 | convolution fusion | flops 10079436800 | bytes 24071296 | tf_op jit(solution)/shard_map/dot_general | solution.py:142
  230.8 0.1 slice.105
  230.9 2.7 %add_convert_fusion = (bf16[800,4,64]{2,0,1:T(8,128)(2,1)}, bf16[800,4,64]{2,0,1:T(8,128)(2,1)}, bf16[800,4,64]{2,0,1:T(8,128)(2,1)}, bf16[800,4,64]{2,0,1:T(8,128)(2,1)}) fusion(f32[800,4,384]{2,0,1:T(8,128)S(1)} %fusion.6, f32[800,64]{1,0:T(8,128)S(1)} %get-tuple-element.15, f32[800,64]{1,0:T(8,128)S(1)} %get-tuple-element.14), kind=kLoop, calls=%fused_computation.18 | loop fusion | flops 3276800 | bytes 5324800 | tf_op jit(solution)/shard_map/convert.3
  233.7 5.8 %concatenate.18 = bf16[800,4,384]{2,0,1:T(8,128)(2,1)S(1)} concatenate(bf16[800,4,64]{2,0,1:T(8,128)(2,1)} %get-tuple-element.4, bf16[800,4,64]{2,0,1:T(8,128)(2,1)} %get-tuple-element.5, bf16[800,4,64]{2,0,1:T(8,128)(2,1)} %get-tuple-element.3, bf16[800,4,64]{2,0,1:T(8,128)(2,1)} %get-tuple-element.2, bf16[800,4,128]{2,0,1:T(8,128)(2,1)S(1)} %slice.105), dimensions={2} | concatenate | bytes 4915200 | tf_op jit(solution)/shard_map/concatenate | solution.py:34
  239.5 0.0 copy-start.2
  239.6 1.4 copy-done.2
  240.9 0.0 slice-start
  240.9 0.2 fusion.52
  241.1 0.2 fusion.22
  241.3 0.6 copy.111
  242.0 0.1 broadcast_in_dim.125
  242.1 1.1 fusion.49
  243.2 0.0 slice-done
  243.2 1.7 fusion.48
  244.9 0.0 copy-start.4
  244.9 2.6 %fusion.53 = (f32[24,4,32]{2,1,0:T(4,128)S(1)}, f32[24,4,32,48]{3,2,1,0:T(8,128)S(1)}) fusion(bf16[24,16,4,128]{3,1,2,0:T(8,128)(2,1)} %get-tuple-element.9, bf16[24,32,4,128]{3,1,0,2:T(8,128)(2,1)} %get-tuple-element.6, pred[24,32,48]{2,1,0:T(8,128)(4,1)S(1)} %and_or_fusion, bf16[24,32,4,128]{3,1,0,2:T(8,128)(2,1)} %get-tuple-element.7), kind=kOutput, calls=%fused_computation.94 | convolution fusion | flops 40845360 | bytes 2605056 | tf_op jit(solution)/shard_map/sub | solution.py:40
  247.5 0.0 copy-done.4
  247.5 0.0 copy-start.1
  247.5 0.9 fusion.11
  248.4 1.0 copy.110
  249.4 0.0 copy-done.1
  (18 shorter events, 0.1 us)
Async XLA Ops:
  7.2 25.5 %copy-start = (bf16[2,32,1024]{2,1,0:T(8,128)(2,1)S(1)}, bf16[2,32,1024]{2,1,0:T(8,128)(2,1)}, u32[]{:S(2)}) copy-start(bf16[2,32,1024]{2,1,0:T(8,128)(2,1)} %param.7) | copy-start | bytes 393220
  8.8 22.5 %all-to-all-start = ((s32[64,1,1]{2,1,0:T(1,128)}), s32[64,1,1]{2,1,0:T(1,128)S(1)}, u32[]{:S(2)}, u32[]{:S(2)}) async-start(s32[64,1,1]{2,1,0:T(1,128)} %copy.58), calls=%async_computation | async-start | bytes 65536 | tf_op jit(solution)/shard_map/all_to_all | solution.py:124
  39.9 100.4 %all-to-all-start.1 = ((bf16[64,1,32,1024]{3,2,1,0:T(8,128)(2,1)}), bf16[64,1,32,1024]{3,2,1,0:T(8,128)(2,1)}, u32[]{:S(2)}, u32[]{:S(2)}) async-start(bf16[64,1,32,1024]{3,2,1,0:T(8,128)(2,1)} %bitcast_select_fusion), calls=%async_computation.1 | async-start | bytes 8388608 | tf_op jit(solution)/shard_map/all_to_all | solution.py:131
  45.6 97.5 %copy-start.5 = (bf16[2,16,1024]{2,1,0:T(8,128)(2,1)S(1)}, bf16[2,16,1024]{2,1,0:T(8,128)(2,1)}, u32[]{:S(2)}) copy-start(bf16[2,16,1024]{2,1,0:T(8,128)(2,1)} %param.6) | copy-start | bytes 196612
  45.6 167.0 %all-gather.2.cloned.1.call-start = ((), (), s32[]{:S(2)}) async-start(), calls=%async_computation.3 | async-start | bytes 8192000 | tf_op jit(solution)/shard_map/all_gather | solution.py:140
  147.0 36.7 %all-to-all-start.2 = ((s32[64,1,1]{2,1,0:T(1,128)}), s32[64,1,1]{2,1,0:T(1,128)S(1)}, u32[]{:S(2)}, u32[]{:S(2)}) async-start(s32[64,1,1]{2,1,0:T(1,128)} %copy.67), calls=%async_computation.2 | async-start | bytes 65536 | tf_op jit(solution)/shard_map/all_to_all | solution.py:132
  166.9 16.7 %copy-start.6 = (bf16[4096]{0:T(1024)(128)(2,1)S(1)}, bf16[4096]{0:T(1024)(128)(2,1)}, u32[]{:S(2)}) copy-start(bf16[4096]{0:T(1024)(128)(2,1)} %param.10) | copy-start | bytes 24580
  212.6 4.7 %copy-start.3 = (bf16[800,4096]{1,0:T(8,128)(2,1)S(1)}, bf16[800,4096]{1,0:T(8,128)(2,1)}, u32[]{:S(2)}) copy-start(bf16[800,4096]{1,0:T(8,128)(2,1)} %all-gather.2.cloned.1.call-done) | copy-start | bytes 19660804
  239.5 1.4 copy-start.2
  240.9 2.2 slice-start
  244.9 2.6 %copy-start.4 = (bf16[24,16,4,128]{3,1,2,0:T(8,128)(2,1)S(1)}, bf16[24,16,4,128]{3,1,2,0:T(8,128)(2,1)}, u32[]{:S(2)}) copy-start(bf16[24,16,4,128]{3,1,2,0:T(8,128)(2,1)} %get-tuple-element.10) | copy-start | bytes 1179652
  247.5 1.9 copy-start.1
Sparse Core Ops, SparseCore 0:
  144.6 67.9 all-gather.1
where the time goes:
time: 257 us; the launch traced here: 256 us
  waiting for transfers between devices  129 us (50%)
  local copies, waits for them, and re-layouts  51.2 us (20%)
  starting transfers between devices  25.9 us (10%)
  other arithmetic  18.1 us (7%)
  matrix products  17.3 us (7%)
  between operations  14.3 us (6%)
    all_to_all x1, waiting for transfers between devices, local(): lax.all_to_all(outgoing, 'store', split_axis=0, concat_axis=0, tiled=True)  94.6 us
    all_gather x1, waiting for transfers between devices, local(): full_rows = lax.all_gather(all_rows, 'tp', axis=1, tiled=True)  26.8 us
    dot_general x1, local copies, waits for them, and re-layouts, local(): raw = jnp.dot(normed, weights_flat, preferred_element_type=jnp.float32)  16.7 us
    unnamed x15, local copies, waits for them, and re-layouts  14.7 us
    dot_general x1, matrix products, local(): raw = jnp.dot(normed, weights_flat, preferred_element_type=jnp.float32)  13.5 us
    all_to_all x1, starting transfers between devices, local(): lax.all_to_all(request, 'store', split_axis=0, concat_axis=0, tiled=True)  13.2 us
    all_to_all x1, waiting for transfers between devices, local(): lax.all_to_all(request, 'store', split_axis=0, concat_axis=0, tiled=True)  7.98 us
    all_to_all x1, starting transfers between devices, local(): lax.all_to_all(out_len, 'store', split_axis=0, concat_axis=0, tiled=True)  7.01 us
  transfers between devices with their start and end apart: 4, of which 3 were waited for; matrix products, arithmetic and copies ran while one was open for 14% of the time, Pallas kernels for 0%

commit v1 on v0

--- a/solution.py
+++ b/solution.py
@@ -137,7 +137,9 @@
     all_rows = jnp.concatenate(
         [query_rows, fetched.reshape(pairs_dev * passage_len, width_part)], axis=0
     )
-    full_rows = lax.all_gather(all_rows, "tp", axis=1, tiled=True)
+    full_rows = jnp.concatenate(
+        lax.all_to_all(jnp.stack([all_rows] * lax.axis_size("tp")), "tp", 0, 0), axis=1
+    )
     normed = rms_rows(full_rows, norm_gain)
     raw = jnp.dot(normed, weights_flat, preferred_element_type=jnp.float32)
     raw = raw.reshape(all_rows.shape[0], heads_part, 3 * head_dim)

time: 257 us -> 301 us (1.17)
  local copies, waits for them, and re-layouts: 51.2 us -> 75.3 us
  waiting for transfers between devices: 129 us -> 148 us
  between operations: 14.3 us -> 0.9 us
  other arithmetic: 18.1 us -> 24.8 us
  starting transfers between devices: 25.9 us -> 31.4 us
    all_to_all x0 -> x1, waiting for transfers between devices: none -> 40.4 us  [local(): lax.all_to_all(jnp.stack([all_rows] * lax.axis_size('tp')), 'tp', 0, 0)]
    all_gather x1 -> x0, waiting for transfers between devices: 26.8 us -> none  [local(): full_rows = lax.all_gather(all_rows, 'tp', axis=1, tiled=True)]
    convert_element_type x0 -> x2, local copies, waits for them, and re-layouts: none -> 24.3 us  [rms_rows(): return scaled.astype(jnp.bfloat16)]
    convert_element_type x1, other arithmetic: 0.01 us -> 7.92 us  [rms_rows(): return scaled.astype(jnp.bfloat16)]
    all_to_all x1, waiting for transfers between devices: 0.01 us -> 6.31 us  [local(): lax.all_to_all(out_len, 'store', split_axis=0, concat_axis=0, tiled=True)]
    all_to_all x0 -> x1, starting transfers between devices: none -> 5.51 us  [local(): lax.all_to_all(jnp.stack([all_rows] * lax.axis_size('tp')), 'tp', 0, 0)]
    another operation x0 -> x1, local copies, waits for them, and re-layouts: none -> 3.67 us  [local(): jnp.stack([all_rows] * lax.axis_size('tp'))]
    unnamed x15 -> x9, local copies, waits for them, and re-layouts: 14.7 us -> 12.5 us
  transfers between devices with their start and end apart: 4 -> 4, of which waited for: 3 -> 4; matrix products, arithmetic and copies ran while one was open for 14% -> 13% of each run, Pallas kernels for 0% -> 0%
where the time goes in v1:
time: 301 us; the launch traced here: 300 us
  waiting for transfers between devices  148 us (49%)
  local copies, waits for them, and re-layouts  75.3 us (25%)
  starting transfers between devices  31.4 us (10%)
  other arithmetic  24.8 us (8%)
  matrix products  18.8 us (6%)
    all_to_all x1, waiting for transfers between devices, local(): lax.all_to_all(outgoing, 'store', split_axis=0, concat_axis=0, tiled=True)  93.9 us
    all_to_all x1, waiting for transfers between devices, local(): lax.all_to_all(jnp.stack([all_rows] * lax.axis_size('tp')), 'tp', 0, 0)  40.4 us
    convert_element_type x2, local copies, waits for them, and re-layouts, rms_rows(): return scaled.astype(jnp.bfloat16)  24.3 us
    dot_general x1, local copies, waits for them, and re-layouts, local(): raw = jnp.dot(normed, weights_flat, preferred_element_type=jnp.float32)  16.7 us
    dot_general x1, matrix products, local(): raw = jnp.dot(normed, weights_flat, preferred_element_type=jnp.float32)  13.6 us
    all_to_all x1, starting transfers between devices, local(): lax.all_to_all(request, 'store', split_axis=0, concat_axis=0, tiled=True)  13.2 us
    unnamed x9, local copies, waits for them, and re-layouts  12.5 us
    convert_element_type x1, other arithmetic, rms_rows(): return scaled.astype(jnp.bfloat16)  7.92 us
  transfers between devices with their start and end apart: 4, of which 4 were waited for; matrix products, arithmetic and copies ran while one was open for 13% of the time, Pallas kernels for 0%

profile of v1, /device:TPU:1, one launch (start us, length us, event | category | flops | bytes accessed | tf_op | source)
XLA Modules:
  0.0 299.7 jit_solution(16836083718970795080)
XLA Ops:
  0.6 0.0 copy-start
  0.6 0.7 and_select_fusion.1
  1.3 0.1 convert_reduce_fusion
  1.4 0.1 select_reduce_fusion
  1.5 0.7 copy.59
  2.3 13.2 %all-to-all-start = ((s32[64,1,1]{2,1,0:T(1,128)}), s32[64,1,1]{2,1,0:T(1,128)S(1)}, u32[]{:S(2)}, u32[]{:S(2)}) async-start(s32[64,1,1]{2,1,0:T(1,128)} %copy.59), calls=%async_computation | async-start | bytes 65536 | tf_op jit(solution)/shard_map/all_to_all | solution.py:124
  15.4 1.4 fusion.47
  16.8 7.9 %all-to-all-done = s32[64,1,1]{2,1,0:T(1,128)S(1)} async-done(((s32[64,1,1]{2,1,0:T(1,128)}), s32[64,1,1]{2,1,0:T(1,128)S(1)}, u32[]{:S(2)}, u32[]{:S(2)}) %all-to-all-start) | async-done | bytes 288 | tf_op jit(solution)/shard_map/all_to_all | solution.py:124
  24.7 0.1 copy.60
  24.8 1.4 compare_select_fusion.5
  26.2 0.0 copy-done
  26.2 2.8 gather_fusion
  29.0 4.5 %bitcast_select_fusion = bf16[64,1,32,1024]{3,2,1,0:T(8,128)(2,1)} fusion(bf16[64,32,1024]{2,1,0:T(8,128)(2,1)} %gather_fusion, pred[64]{0:T(512)(128)(4,1)S(1)} %compare_bitcast_fusion), kind=kLoop, calls=%fused_computation.11 | loop fusion | flops 2097152 | bytes 8388672 | tf_op jit(solution)/shard_map/jit(_where)/select_n | solution.py:127
  33.5 5.7 %all-to-all-start.1 = ((bf16[64,1,32,1024]{3,2,1,0:T(8,128)(2,1)}), bf16[64,1,32,1024]{3,2,1,0:T(8,128)(2,1)}, u32[]{:S(2)}, u32[]{:S(2)}) async-start(bf16[64,1,32,1024]{3,2,1,0:T(8,128)(2,1)} %bitcast_select_fusion), calls=%async_computation.1 | async-start | bytes 8388608 | tf_op jit(solution)/shard_map/all_to_all | solution.py:131
  39.2 0.0 copy-start.2
  39.2 0.7 copy.69
  39.9 93.9 %all-to-all-done.1 = bf16[64,1,32,1024]{3,2,1,0:T(8,128)(2,1)} async-done(((bf16[64,1,32,1024]{3,2,1,0:T(8,128)(2,1)}), bf16[64,1,32,1024]{3,2,1,0:T(8,128)(2,1)}, u32[]{:S(2)}, u32[]{:S(2)}) %all-to-all-start.1) | async-done | bytes 4194336 | tf_op jit(solution)/shard_map/all_to_all | solution.py:131
  133.8 7.0 %all-to-all-start.3 = ((s32[64,1,1]{2,1,0:T(1,128)}), s32[64,1,1]{2,1,0:T(1,128)S(1)}, u32[]{:S(2)}, u32[]{:S(2)}) async-start(s32[64,1,1]{2,1,0:T(1,128)} %copy.69), calls=%async_computation.3 | async-start | bytes 65536 | tf_op jit(solution)/shard_map/all_to_all | solution.py:132
  140.8 2.8 gather_fusion.1
  143.7 0.0 copy-done.2
  143.7 0.1 pad_maximum_fusion
  143.8 6.3 %all-to-all-done.3 = s32[64,1,1]{2,1,0:T(1,128)S(1)} async-done(((s32[64,1,1]{2,1,0:T(1,128)}), s32[64,1,1]{2,1,0:T(1,128)S(1)}, u32[]{:S(2)}, u32[]{:S(2)}) %all-to-all-start.3) | async-done | bytes 288 | tf_op jit(solution)/shard_map/all_to_all | solution.py:132
  150.2 3.7 %stack.2 = bf16[4,800,1024]{2,1,0:T(8,128)(2,1)} broadcast(bf16[800,1024]{1,0:T(8,128)(2,1)S(1)} %pad_maximum_fusion), dimensions={1,2} | broadcast | bytes 8192000 | tf_op jit(solution)/shard_map/stack | solution.py:141
  153.8 0.0 copy-start.3
  153.8 5.5 %all-to-all-start.2 = ((bf16[4,800,1024]{2,1,0:T(8,128)(2,1)}), bf16[4,800,1024]{2,1,0:T(8,128)(2,1)}, u32[]{:S(2)}, u32[]{:S(2)}) async-start(bf16[4,800,1024]{2,1,0:T(8,128)(2,1)} %stack.2), calls=%async_computation.2 | async-start | bytes 13107200 | tf_op jit(solution)/shard_map/all_to_all | solution.py:141
  159.3 0.0 copy-done.3
  159.4 12.5 %copy.84 = bf16[512,8,4,384]{3,1,2,0:T(8,128)(2,1)} copy(bf16[512,8,4,384]{3,2,1,0:T(4,128)(2,1)} %bitcast.43) | data formatting | bytes 25165824
  171.9 16.7 %copy.63 = bf16[1536,4096]{1,0:T(8,128)(2,1)} copy(bf16[1536,4096]{0,1:T(8,128)(2,1)} %bitcast.42) | data formatting | bytes 25165824 | tf_op jit(solution)/shard_map/dot_general | solution.py:144
  188.6 0.1 add.65
  188.7 0.1 tile.7
  188.8 0.1 pad_maximum_fusion.1
  188.9 1.5 multiply_cosine_fusion
  190.4 1.2 reduce.3
  191.6 0.7 gather_fusion.2
  192.3 0.1 iota_compare_fusion.1
  192.4 0.1 broadcast_compare_fusion
  192.4 0.1 and_or_fusion
  192.5 40.4 %all-to-all-done.2 = bf16[4,800,1024]{2,1,0:T(8,128)(2,1)} async-done(((bf16[4,800,1024]{2,1,0:T(8,128)(2,1)}), bf16[4,800,1024]{2,1,0:T(8,128)(2,1)}, u32[]{:S(2)}, u32[]{:S(2)}) %all-to-all-start.2) | async-done | bytes 6553632 | tf_op jit(solution)/shard_map/all_to_all | solution.py:141
  232.9 4.2 %fusion.2 = f32[800]{0:T(1024)S(1)} fusion(bf16[4,800,1024]{2,1,0:T(8,128)(2,1)} %all-to-all-done.2), kind=kLoop, calls=%fused_computation.7 | loop fusion | flops 9829600 | bytes 6556800 | tf_op jit(solution)/shard_map/reduce_sum | solution.py:10
  237.1 7.9 %fusion.5 = bf16[800,4,1024]{2,0,1:T(8,128)(2,1)} fusion(bf16[4,800,1024]{2,1,0:T(8,128)(2,1)} %all-to-all-done.2, f32[4,1024]{1,0:T(4,128)S(1)} %reshape.350, f32[800]{0:T(1024)S(1)} %add_rsqrt_fusion), kind=kLoop, calls=%fused_computation.10 | loop fusion | flops 13107200 | bytes 13126784 | tf_op jit(solution)/shard_map/convert_element_type | solution.py:12
  245.0 10.6 %copy.62 = bf16[800,4,1024]{2,1,0:T(4,128)(2,1)} copy(bf16[800,4,1024]{2,0,1:T(8,128)(2,1)} %fusion.5) | data formatting | bytes 13107200 | tf_op jit(solution)/shard_map/convert_element_type | solution.py:12
  255.7 13.7 %reshape.387 = bf16[800,4096,1]{1,0,2:T(8,128)(2,1)} reshape(bf16[800,4,1024]{2,1,0:T(4,128)(2,1)} %copy.62) | data formatting | bytes 13107200 | tf_op jit(solution)/shard_map/convert_element_type | solution.py:12
  269.3 13.6 %fusion.58 = f32[800,4,384]{2,0,1:T(8,128)S(1)} fusion(bf16[800,4096,1]{1,0,2:T(8,128)(2,1)} %reshape.387, bf16[4,384,4096]{2,1,0:T(8,128)(2,1)} %bitcast.44), kind=kOutput, calls=%fused_computation.92 | convolution fusion | flops 10066329600 | bytes 24051712 | tf_op jit(solution)/shard_map/dot_general | solution.py:144
  282.9 0.1 slice.105
  283.0 2.7 add_convert_fusion
  285.8 5.8 %concatenate.18 = bf16[800,4,384]{2,0,1:T(8,128)(2,1)S(1)} concatenate(bf16[800,4,64]{2,0,1:T(8,128)(2,1)} %get-tuple-element.4, bf16[800,4,64]{2,0,1:T(8,128)(2,1)} %get-tuple-element.5, bf16[800,4,64]{2,0,1:T(8,128)(2,1)} %get-tuple-element.3, bf16[800,4,64]{2,0,1:T(8,128)(2,1)} %get-tuple-element.2, bf16[800,4,128]{2,0,1:T(8,128)(2,1)S(1)} %slice.105), dimensions={2} | concatenate | bytes 4915200 | tf_op jit(solution)/shard_map/concatenate | solution.py:34
  291.6 0.2 slice.89
  291.9 0.5 fusion.44
  292.5 0.1 broadcast_in_dim.125
  292.6 0.2 fusion.45
  292.8 2.8 fusion.49
  295.5 0.0 copy-start.1
  295.5 2.1 fusion.7
  297.6 1.0 copy.112
  298.6 0.2 fusion.48
  298.8 0.2 fusion.18
  299.0 0.6 copy.113
  299.7 0.0 copy-done.1
  (18 shorter events, 0.2 us)
Async XLA Ops:
  0.6 25.5 %copy-start = (bf16[2,32,1024]{2,1,0:T(8,128)(2,1)S(1)}, bf16[2,32,1024]{2,1,0:T(8,128)(2,1)}, u32[]{:S(2)}) copy-start(bf16[2,32,1024]{2,1,0:T(8,128)(2,1)} %param.7) | copy-start | bytes 393220
  2.3 22.5 %all-to-all-start = ((s32[64,1,1]{2,1,0:T(1,128)}), s32[64,1,1]{2,1,0:T(1,128)S(1)}, u32[]{:S(2)}, u32[]{:S(2)}) async-start(s32[64,1,1]{2,1,0:T(1,128)} %copy.59), calls=%async_computation | async-start | bytes 65536 | tf_op jit(solution)/shard_map/all_to_all | solution.py:124
  33.5 100.4 %all-to-all-start.1 = ((bf16[64,1,32,1024]{3,2,1,0:T(8,128)(2,1)}), bf16[64,1,32,1024]{3,2,1,0:T(8,128)(2,1)}, u32[]{:S(2)}, u32[]{:S(2)}) async-start(bf16[64,1,32,1024]{3,2,1,0:T(8,128)(2,1)} %bitcast_select_fusion), calls=%async_computation.1 | async-start | bytes 8388608 | tf_op jit(solution)/shard_map/all_to_all | solution.py:131
  39.2 104.5 %copy-start.2 = (bf16[2,16,1024]{2,1,0:T(8,128)(2,1)S(1)}, bf16[2,16,1024]{2,1,0:T(8,128)(2,1)}, u32[]{:S(2)}) copy-start(bf16[2,16,1024]{2,1,0:T(8,128)(2,1)} %param.6) | copy-start | bytes 196612
  133.8 16.3 %all-to-all-start.3 = ((s32[64,1,1]{2,1,0:T(1,128)}), s32[64,1,1]{2,1,0:T(1,128)S(1)}, u32[]{:S(2)}, u32[]{:S(2)}) async-start(s32[64,1,1]{2,1,0:T(1,128)} %copy.69), calls=%async_computation.3 | async-start | bytes 65536 | tf_op jit(solution)/shard_map/all_to_all | solution.py:132
  153.8 5.5 %copy-start.3 = (bf16[4096]{0:T(1024)(128)(2,1)S(1)}, bf16[4096]{0:T(1024)(128)(2,1)}, u32[]{:S(2)}) copy-start(bf16[4096]{0:T(1024)(128)(2,1)} %param.10) | copy-start | bytes 24580
  153.8 79.1 %all-to-all-start.2 = ((bf16[4,800,1024]{2,1,0:T(8,128)(2,1)}), bf16[4,800,1024]{2,1,0:T(8,128)(2,1)}, u32[]{:S(2)}, u32[]{:S(2)}) async-start(bf16[4,800,1024]{2,1,0:T(8,128)(2,1)} %stack.2), calls=%async_computation.2 | async-start | bytes 13107200 | tf_op jit(solution)/shard_map/all_to_all | solution.py:141
  295.5 4.1 %copy-start.1 = (bf16[2,32,1024]{2,1,0:T(8,128)(2,1)S(1)}, bf16[2,32,1024]{2,1,0:T(8,128)(2,1)}, u32[]{:S(2)}) copy-start(bf16[2,32,1024]{2,1,0:T(8,128)(2,1)} %param.7) | copy-start | bytes 393220
